TPU v7x, 256 devices: a whole 4x4x8 slice. The times are simulated.
256 devices in a mesh: tm: 8 (over z_hi, core), space: 32 (over x, z_lo, y).
Axes of the slice: x: 4, y: 4, z: 8 (z_hi: 4, z_lo: 2; z = z_hi * 2 + z_lo), core: 2. Of those that a mesh axis runs over, the one named last changes fastest.
Arguments:
- dual_state: float32 [800, 16, 4, 1024], P('space', 'tm'), may hold values from -6 to 6
- obs_dual: float32 [800, 16, 4, 1024], P('space', 'tm'), may hold values from -6 to 6
- increment: float32 [800, 16, 4, 1024], P('space', 'tm'), may hold values from -6 to 6
- wind_east: float32 [800, 16, 1024], P('space', 'tm'), may hold values from -0.45 to 0.45
- wind_north: float32 [800, 16, 1024], P('space', 'tm'), may hold values from -0.45 to 0.45
- deviation: float32 [800, 4, 1024], P('space'), may hold values from 0.1 to 1
- merid_filter: float32 [800, 800], replicated, may hold values from -1 to 2
- obs_weight: float32 [800, 16, 4, 1024], P('space', 'tm'), may hold values from 0 to 1
- obs_error: float32 [800, 16, 4, 1024], P('space', 'tm'), may hold values from 0.25 to 2.5
Outputs:
- precond_dual: float32 [800, 16, 4, 1024], P('space', 'tm')
- precond_obs: float32 [800, 16, 4, 1024], P('space', 'tm')
- precond_increment: float32 [800, 16, 4, 1024], P('space', 'tm')
All inputs are finite; a program needn't handle non-finite values.
Results may differ from a plain program's by a relative error of at most 0.000075.
Values sent between devices are 32-bit elements; how exact they have to be, the bound alone decides.
No kernel may reach another device: no remote copies, remote signals or barrier semaphores. Data moves between devices by JAX's collectives and lax.ppermute only.
A program may use at most 64 MiB of HBM per device.

v0:
```python
import functools

import jax
import jax.numpy as jnp
from jax import lax
from jax.experimental import pallas as pl
from jax.experimental.pallas import tpu as pltpu
from jax.sharding import PartitionSpec as P

ROWS, SUBS, FIELDS, LON = 25, 2, 4, 1024
LAT = 800
SPACE = 32
CHIPS = 4
BLOCK = 400
LANES = 128
TILES = LON // LANES
VMEM_LIMIT = 16 * 1024 * 1024
WHOLE_VMEM = 61 * 1024 * 1024
OBS_FLOPS = 10**11
SUM_FLOPS = 10**11

F32 = jnp.float32
BF16 = jnp.bfloat16
TOKEN = jax.ShapeDtypeStruct((8, LANES), F32)


HBM = pl.BlockSpec(memory_space=pltpu.HBM)
VMEM = pl.BlockSpec(memory_space=pltpu.VMEM)


def call(
    kernel, outs, operands, scratch=(), after=(), flops=0, far_ins=(), far_outs=(),
    limit=VMEM_LIMIT,
):
    count, made = len(operands), len(outs)

    def run(*refs):
        begin = count + len(after)
        kernel(*refs[:count], *refs[begin : begin + made], *refs[begin + made + 1 :])

    size = sum(4 * a.size for a in operands) + sum(4 * o.size for o in outs)
    return pl.pallas_call(
        run,
        out_shape=(*outs, TOKEN),
        in_specs=[HBM if k in far_ins else VMEM for k in range(count)] + [HBM] * len(after),
        out_specs=(*(HBM if k in far_outs else VMEM for k in range(made)), HBM),
        scratch_shapes=list(scratch),
        compiler_params=pltpu.CompilerParams(vmem_limit_bytes=limit),
        cost_estimate=pl.CostEstimate(flops=flops, bytes_accessed=size, transcendentals=0),
    )(*operands, *after)


def hold(array, after=(), flops=0):
    def run(*refs):
        pass

    return pl.pallas_call(
        run,
        out_shape=field(*array.shape),
        in_specs=[pl.BlockSpec(memory_space=pl.ANY)] * (1 + len(after)),
        out_specs=pl.BlockSpec(memory_space=pl.ANY),
        input_output_aliases={0: 0},
        compiler_params=pltpu.CompilerParams(vmem_limit_bytes=1024 * 1024),
        cost_estimate=pl.CostEstimate(flops=flops, bytes_accessed=0, transcendentals=0),
    )(array, *after)


def place():
    return lax.axis_index("tm")


def rows_loop(begin, end, unroll, each, then=None):
    @pl.loop(0, (end - begin) // unroll)
    def _(group):
        for k in range(unroll):
            each(begin + group * unroll + k)
        if then is not None:
            then(group)

    for row in range(end - (end - begin) % unroll, end):
        each(row)


GROUP = 5
GROUPS = ROWS // GROUP


def group_rows(group):
    return pl.ds(group * GROUP, GROUP)


def field(*shape):
    return jax.ShapeDtypeStruct(shape, F32)


def split(x):
    high = x.astype(BF16)
    return high, (x - high.astype(F32)).astype(BF16)


def dot3(a_high, a_low, b_high, b_low, dims):
    def one(a, b):
        return lax.dot_general(a, b, (dims, ((), ())), preferred_element_type=F32)

    return one(a_high, b_high) + (one(a_high, b_low) + one(a_low, b_high))


def edge_kernel(
    inc_ref,
    dual_ref,
    east_ref,
    north_ref,
    up_ref,
    down_ref,
    wind_ref,
    ahead_ref,
    inc_rows,
    dual_rows,
    east_rows,
    north_rows,
    done,
):
    copies = [
        pltpu.make_async_copy(east_ref, east_rows, done.at[2, 0]),
        pltpu.make_async_copy(north_ref, north_rows, done.at[2, 1]),
    ]
    for k, rows in enumerate((pl.ds(0, 2), pl.ds(ROWS - 2, 2))):
        copies += [
            pltpu.make_async_copy(inc_ref.at[rows], inc_rows.at[k], done.at[k, 0]),
            pltpu.make_async_copy(dual_ref.at[rows], dual_rows.at[k], done.at[k, 1]),
        ]
    for copy in copies:
        copy.start()
    for copy in copies:
        copy.wait()

    for side, (target, begin) in enumerate(((down_ref, 0), (up_ref, ROWS - 2))):
        for k in range(2):
            for sub in range(SUBS):
                start = 8 * k + FIELDS * sub
                target[start : start + FIELDS, :] = dual_rows[side, k, sub]
                target[24 + start : 24 + start + FIELDS, :] = inc_rows[side, k, sub]
                at = 16 + 4 * k + 2 * sub
                target[at : at + 1, :] = east_rows[begin + k, sub : sub + 1]
                target[at + 1 : at + 2, :] = north_rows[begin + k, sub : sub + 1]

    def each(row):
        east, north = east_rows[row], north_rows[row]
        wind_ref[row, 0:1] = east[0:1]
        wind_ref[row, 1:2] = north[0:1]
        wind_ref[row, 2:3] = east[1:2]
        wind_ref[row, 3:4] = north[1:2]
        ahead_ref[row, 0:1] = east[1:2]
        ahead_ref[row, 1:2] = north[1:2]

    rows_loop(0, ROWS, GROUP, each)


def edges(increment, dual_state, wind_east, wind_north):
    ends = pltpu.VMEM((2, 2, SUBS, FIELDS, LON), F32)
    wind = pltpu.VMEM((ROWS, SUBS, LON), F32)
    return call(
        edge_kernel,
        [field(40, LON)] * 2 + [field(ROWS, 4, LON), field(ROWS, 2, LON)],
        [increment, dual_state, wind_east, wind_north],
        [ends, ends, wind, wind, pltpu.SemaphoreType.DMA((3, 2))],
        far_ins=(0, 1, 2, 3),
        limit=WHOLE_VMEM,
    )


def rim_kernel(low_ref, high_ref, rim_ref):
    for k in range(2):
        rim_ref[2 * k : 2 * k + 2, :] = low_ref[18 + 4 * k : 20 + 4 * k, :]
        rim_ref[4 + 2 * k : 6 + 2 * k, :] = high_ref[18 + 4 * k : 20 + 4 * k, :]


def square_kernel(begin, w_ref, high_ref, low_ref, w_high, w_low):
    high, low = split(w_ref[...])
    w_high[...] = high
    w_low[...] = low
    rows = slice(begin, begin + BLOCK)
    product = dot3(w_high[rows, :], w_low[rows, :], w_high[...], w_low[...], ((1,), (1,)))
    product_high, product_low = split(product)
    high_ref[...] = product_high
    low_ref[...] = product_low


def filter_kernel(
    first_high, first_low, second_high, second_low, x_ref, y_ref, high, low, x_high, x_low, y_rows,
    done, sent,
):
    copies = [
        pltpu.make_async_copy(source, target.at[pl.ds(block * BLOCK, BLOCK)], done.at[k, block])
        for block, pair in enumerate(((first_high, first_low), (second_high, second_low)))
        for k, (source, target) in enumerate(zip(pair, (high, low)))
    ]
    for copy in copies:
        copy.start()
    for part in range(2):
        part_high, part_low = split(x_ref[pl.ds(part, LAT, stride=2), :])
        x_high[:, part * LANES : (part + 1) * LANES] = part_high
        x_low[:, part * LANES : (part + 1) * LANES] = part_low
    for copy in copies:
        copy.wait()

    def sending(block):
        rows = pl.ds(pl.multiple_of(2 * block * BLOCK, 2 * BLOCK), 2 * BLOCK)
        return pltpu.make_async_copy(y_rows.at[rows], y_ref.at[rows], sent.at[block])

    @pl.loop(0, LAT // BLOCK)
    def _(block):
        rows = pl.ds(pl.multiple_of(block * BLOCK, BLOCK), BLOCK)
        product = dot3(high[rows, :], low[rows, :], x_high[...], x_low[...], ((1,), (0,)))
        for part in range(2):
            y_rows[pl.ds(2 * block * BLOCK + part, BLOCK, stride=2), :] = product[
                :, part * LANES : (part + 1) * LANES
            ]
        sending(block).start()

    @pl.loop(0, LAT // BLOCK)
    def _(block):
        sending(block).wait()


def paired(first, second):
    lower = lax.broadcasted_iota(jnp.int32, (2 * FIELDS, LON), 0) < FIELDS
    shape = (2 * FIELDS, LON)
    return jnp.where(lower, jnp.broadcast_to(first, shape), jnp.broadcast_to(second, shape))


def tangent_row(below, here, above, east, north):
    east_size, north_size = jnp.abs(east), jnp.abs(north)
    along = jnp.where(east > 0, pltpu.roll(here, 1, 1), pltpu.roll(here, LON - 1, 1))
    across = jnp.where(north > 0, below, above)
    return (1.0 - east_size - north_size) * here + east_size * along + north_size * across


def halo_rows(target, source, low, high):
    for k in range(2):
        target[k] = low[24 + 8 * k : 32 + 8 * k, :]
        target[ROWS + 2 + k] = high[24 + 8 * k : 32 + 8 * k, :]

    def each(row):
        target[row + 2] = jnp.concatenate([source[row, 0], source[row, 1]], axis=0)

    rows_loop(0, ROWS, 5, each)


def tangent_kernel(
    inc_ref,
    low_ref,
    high_ref,
    wind_ref,
    base_ref,
    total_ref,
    rows_ref,
    step_ref,
    east_ref,
    north_ref,
):
    halo_rows(rows_ref, inc_ref, low_ref, high_ref)

    def spread(row, block):
        east_ref[row] = paired(block[0:1], block[2:3])
        north_ref[row] = paired(block[1:2], block[3:4])

    spread(1, low_ref[20:24, :])
    spread(ROWS + 2, high_ref[16:20, :])
    rows_loop(0, ROWS, 5, lambda row: spread(row + 2, wind_ref[row]))

    def first_step(row):
        step_ref[row] = tangent_row(
            rows_ref[row - 1], rows_ref[row], rows_ref[row + 1], east_ref[row], north_ref[row]
        )

    rows_loop(1, ROWS + 3, 3, first_step)

    def second_step(row):
        advanced = tangent_row(
            step_ref[row + 1], step_ref[row + 2], step_ref[row + 3],
            east_ref[row + 2], north_ref[row + 2],
        )
        first = inc_ref[row, 0]
        second = first + inc_ref[row, 1] - advanced[0:4]
        base_ref[row, 0] = first
        base_ref[row, 1] = second
        total_ref[row] = second - advanced[4:8]

    rows_loop(0, ROWS, 5, second_step)


def adjoint_parts(here, east, north):
    along, across = east * here, north * here
    zero = jnp.zeros_like(here)
    kept = (1.0 - jnp.abs(east) - jnp.abs(north)) * here
    kept = kept + pltpu.roll(jnp.where(east > 0, along, zero), LON - 1, 1)
    kept = kept + pltpu.roll(jnp.where(east > 0, zero, -along), 1, 1)
    to_south = jnp.where(north > 0, across, zero)
    to_north = jnp.where(north > 0, zero, -across)
    return kept, to_south, to_north


def third_kernel(dual_ref, obs_ref, weight_ref, rows_ref, third_ref):
    def each(row):
        first, second = dual_ref[row, 0], dual_ref[row, 1]
        rows_ref[row] = jnp.concatenate([first, second], axis=0)
        third_ref[row, 0] = first + weight_ref[row, 0] * obs_ref[row, 0]
        third_ref[row, 1] = second + weight_ref[row, 1] * obs_ref[row, 1]

    rows_loop(0, ROWS, GROUP, each)


def adjoint_kernel(
    own_ref,
    third_ref,
    wind_ref,
    low_ref,
    high_ref,
    ahead_ref,
    rim_ref,
    base_ref,
    sums_ref,
    keep_ref,
    send_ref,
    rows_ref,
    step_ref,
    back_ref,
    east_ref,
    north_ref,
):
    def spread(row, early, block):
        east_ref[row] = paired(early[0:1], block[0:1])
        north_ref[row] = paired(early[1:2], block[1:2])

    for k in range(2):
        at = 16 + 4 * k
        spread(k, rim_ref[2 * k : 2 * k + 2, :], low_ref[at : at + 2, :])
        spread(ROWS + 2 + k, rim_ref[4 + 2 * k : 6 + 2 * k, :], high_ref[at : at + 2, :])
    rows_loop(0, ROWS, 5, lambda row: spread(row + 2, ahead_ref[row], wind_ref[row]))
    rows_ref[2 : ROWS + 2] = own_ref[...]
    for k in range(2):
        rows_ref[k] = low_ref[8 * k : 8 * k + 8, :]
        rows_ref[ROWS + 2 + k] = high_ref[8 * k : 8 * k + 8, :]

    def sweep(source, target, begin, end, unroll):
        def parts(row):
            return adjoint_parts(source[row], east_ref[row], north_ref[row])

        def step(group, carry):
            pending, from_below = carry
            for k in range(unroll):
                row = begin + 1 + group * unroll + k
                kept, to_south, to_north = parts(row)
                target[row - 1] = pending + to_south
                pending, from_below = kept + from_below, to_north
            return pending, from_below

        kept, _, to_north = parts(begin)
        lax.fori_loop(0, (end - begin - 1) // unroll, step, (kept, to_north))

    sweep(rows_ref, step_ref, 0, ROWS + 4, 4)
    sweep(step_ref, back_ref, 1, ROWS + 3, 2)

    here = place().astype(F32)
    inner = jnp.minimum(here, 1.0)
    is_first = place() % 2 == 0

    def each(row):
        returned = back_ref[row + 2]
        before = inner * returned[0:4]
        dual_first, dual_second = own_ref[row, 0:4], own_ref[row, 4:8]
        third_first, third_second = third_ref[row, 0], third_ref[row, 1]
        base = third_first - returned[4:8] + third_second
        base_ref[row, 0] = base
        base_ref[row, 1] = third_second
        sums = dual_first + (2.0 * here) * before - (2.0 * here + 1.0) * base
        total = sums + dual_second - third_second
        sums_ref[row, 0] = sums
        sums_ref[row, 1] = total
        later = base - before
        keep_ref[row] = jnp.where(is_first, later, total)
        send_ref[row] = jnp.where(is_first, total, later)

    rows_loop(0, ROWS, GROUP, each)


def spread_kernel(
    base_ref,
    sums_ref,
    deviation_ref,
    carry_ref,
    received_ref,
    other_ref,
    total_ref,
    total_received_ref,
    dual_ref,
    column_ref,
    model_ref,
):
    here = place().astype(F32)
    is_first = place() % 2 == 0

    def each(row):
        own, other = carry_ref[row] + received_ref[row], other_ref[row]
        later = jnp.where(is_first, own, other)
        earlier = jnp.where(is_first, other, own)
        deviation = deviation_ref[row]
        for sub in range(SUBS):
            dual_ref[row, sub] = base_ref[row, sub] + later
            sums = earlier + sums_ref[row, sub] - (2.0 * here + (1.0 + sub)) * later
            scaled = deviation * sums
            for pair in range(2):
                for tile in range(TILES):
                    column_ref[sub * 16 + pair * 8 + tile, row] = scaled[
                        2 * pair : 2 * pair + 2, tile * LANES : (tile + 1) * LANES
                    ]
        model_ref[row] = total_ref[row] + total_received_ref[row]

    rows_loop(0, ROWS, GROUP, each)


def obs_kernel(
    obs_far, inc_far, weight_far, error_far, out_far, obs, inc, weight, error, out, done, sent
):
    def copies(group):
        rows = group_rows(group)
        return [
            pltpu.make_async_copy(far.at[rows], near.at[rows], done.at[k, group])
            for k, (far, near) in enumerate(
                ((obs_far, obs), (inc_far, inc), (weight_far, weight), (error_far, error))
            )
        ]

    def sending(group):
        rows = group_rows(group)
        return pltpu.make_async_copy(out.at[rows], out_far.at[rows], sent.at[group])

    for group in range(GROUPS):
        for copy in copies(group):
            copy.start()

    @pl.loop(0, GROUPS)
    def _(group):
        for copy in copies(group):
            copy.wait()
        for k in range(GROUP):
            row = group * GROUP + k
            scale = error[row]
            out[row] = (scale * obs[row] + weight[row] * inc[row]) / scale
        sending(group).start()

    @pl.loop(0, GROUPS)
    def _(group):
        sending(group).wait()


def sum_kernel(*refs):
    def each(row):
        total = refs[0][row]
        for ref in refs[1:-1]:
            total = total + ref[row]
        refs[-1][row] = total

    rows_loop(0, ROWS, GROUP, each)


def finish_kernel(
    column_ref,
    base_ref,
    deviation_ref,
    own_ref,
    other_ref,
    received_ref,
    out_ref,
    out_rows,
    done,
):
    is_first = place() % 2 == 0

    def each(row):
        received = received_ref[row]
        earlier = own_ref[row] + other_ref[row]
        earlier = earlier + jnp.where(is_first, jnp.zeros_like(received), received)
        deviation = deviation_ref[row]
        for sub in range(SUBS):
            filtered = jnp.concatenate(
                [
                    jnp.concatenate(
                        [column_ref[sub * 16 + pair * 8 + tile, row] for tile in range(TILES)],
                        axis=1,
                    )
                    for pair in range(2)
                ],
                axis=0,
            )
            out_rows[row, sub] = deviation * filtered + (base_ref[row, sub] + earlier)

    def copy(group):
        rows = group_rows(group)
        return pltpu.make_async_copy(out_rows.at[rows], out_ref.at[rows], done.at[group])

    rows_loop(0, ROWS, GROUP, each, lambda group: copy(group).start())

    @pl.loop(0, GROUPS)
    def _(group):
        copy(group).wait()


def body(
    dual_state,
    obs_dual,
    increment,
    wind_east,
    wind_north,
    deviation,
    merid_filter,
    obs_weight,
    obs_error,
):
    size = lax.axis_size("space")
    upward = [(i, i + 1) for i in range(size - 1)]
    downward = [(i + 1, i) for i in range(size - 1)]
    following = [(i, i + 1) for i in range(2 * CHIPS - 1)]
    swap = [(i, i ^ 1) for i in range(2 * CHIPS)]

    def by_core(first, second):
        return [(2 * a, 2 * b) for a, b in first] + [(2 * a + 1, 2 * b + 1) for a, b in second]

    rise = [(c, c + 1) for c in range(CHIPS - 1)]
    fall = [(c + 1, c) for c in range(CHIPS - 1)]
    ends = (0, CHIPS - 1)
    whole, half = field(ROWS, SUBS, FIELDS, LON), field(ROWS, FIELDS, LON)

    to_north, to_south, winds, ahead, _ = edges(increment, dual_state, wind_east, wind_north)
    low = lax.ppermute(to_north, "space", upward)
    high = lax.ppermute(to_south, "space", downward)
    ahead = lax.ppermute(ahead, "tm", following)
    extended = pltpu.VMEM((ROWS + 4, 8, LON), F32)
    whole_rows = pltpu.VMEM((ROWS, SUBS, FIELDS, LON), F32)
    own_rows, third, token = call(
        third_kernel,
        [field(ROWS, 8, LON), whole],
        [dual_state, obs_dual, obs_weight],
        flops=4 * ROWS * 8 * LON,
    )
    rim, _ = call(rim_kernel, [field(8, LON)], [low, high], after=[token])
    rim = lax.ppermute(rim, "tm", following)
    model_base, model_total, token = call(
        tangent_kernel,
        [whole, half],
        [increment, low, high, winds],
        [extended] * 4,
        flops=40 * ROWS * 8 * LON,
    )
    dual_base, dual_sums, keep, send, _ = call(
        adjoint_kernel,
        [whole, whole, half, half],
        [own_rows, third, winds, low, high, ahead, rim],
        [extended] * 5,
        after=[token],
        flops=60 * ROWS * 8 * LON,
    )

    received = lax.ppermute(send, "tm", swap)
    chip_total, token = call(sum_kernel, [half], [keep, received], flops=ROWS * 4 * LON)
    near = lax.ppermute(chip_total, "tm", by_core(fall, rise))
    wrapped = lax.ppermute(chip_total, "tm", by_core([ends[::-1]], [ends]))

    square = pltpu.VMEM((LAT, LAT), BF16)

    def square_half(begin, after):
        return call(
            functools.partial(square_kernel, begin),
            [jax.ShapeDtypeStruct((BLOCK, LAT), BF16)] * 2,
            [merid_filter],
            [square] * 2,
            after=after,
            flops=3 * LAT**3,
        )

    first_high, first_low, token = square_half(0, [token])
    near = hold(near, [token])
    on = lax.ppermute(near, "tm", by_core(fall[:2], rise[1:]))
    second_high, second_low, token = square_half(BLOCK, [near])
    model_received = lax.ppermute(model_total, "tm", swap)

    carry, _ = call(
        sum_kernel, [half], [near, wrapped, on], after=[token], flops=2 * ROWS * 4 * LON
    )
    other = lax.ppermute(carry, "tm", swap)

    precond_dual, columns, model_chip, token = call(
        spread_kernel,
        [whole, field(SPACE, ROWS, 2, LANES), half],
        [
            dual_base,
            dual_sums,
            deviation,
            carry,
            received,
            other,
            model_total,
            model_received,
        ],
        flops=10 * ROWS * 8 * LON,
    )

    columns = lax.all_to_all(columns, "space", split_axis=0, concat_axis=0, tiled=True)
    model_near = lax.ppermute(model_chip, "tm", by_core([ends], rise))

    precond_obs, token = call(
        obs_kernel,
        [whole],
        [obs_dual, increment, obs_weight, obs_error],
        [whole_rows] * 5
        + [pltpu.SemaphoreType.DMA((4, GROUPS)), pltpu.SemaphoreType.DMA((GROUPS,))],
        after=[precond_dual],
        flops=OBS_FLOPS,
        far_ins=(0, 1, 2, 3),
        far_outs=(0,),
        limit=WHOLE_VMEM,
    )

    columns, token = call(
        filter_kernel,
        [field(2 * LAT, LANES)],
        [first_high, first_low, second_high, second_low, columns.reshape(2 * LAT, LANES)],
        [square] * 2
        + [pltpu.VMEM((LAT, 2 * LANES), BF16)] * 2
        + [pltpu.VMEM((2 * LAT, LANES), F32), pltpu.SemaphoreType.DMA((2, LAT // BLOCK))]
        + [pltpu.SemaphoreType.DMA((LAT // BLOCK,))],
        after=[token, model_near],
        flops=6 * LAT * LAT * 2 * LANES,
        far_ins=(0, 1, 2, 3),
        far_outs=(0,),
        limit=63 * 1024 * 1024,
    )
    columns = lax.all_to_all(
        columns.reshape(SPACE, ROWS, 2, LANES), "space", split_axis=0, concat_axis=0, tiled=True
    )

    model_on = lax.ppermute(model_near, "tm", by_core([], rise[1:]))
    model_carry, _ = call(
        sum_kernel, [half], [model_near, model_on], after=[token], flops=SUM_FLOPS
    )
    model_other = lax.ppermute(model_carry, "tm", swap)

    precond_increment, _ = call(
        finish_kernel,
        [whole],
        [columns, model_base, deviation, model_carry, model_other, model_received],
        [whole_rows, pltpu.SemaphoreType.DMA((GROUPS,))],
        flops=4 * ROWS * 8 * LON,
        far_outs=(0,),
    )
    return (precond_dual, precond_obs, precond_increment)


def solution(mesh):
    banded = P("space", "tm", None, None)
    placed = (
        banded,
        banded,
        banded,
        P("space", "tm", None),
        P("space", "tm", None),
        P("space", None, None),
        P(),
        banded,
        banded,
    )
    return jax.shard_map(
        body,
        mesh=mesh,
        in_specs=placed,
        out_specs=(banded, banded, banded),
        check_vma=False,
    )
```

profile of v0, /device:TPU:8, one launch (start us, length us, event | category | flops | bytes accessed | tf_op | source)
XLA Modules:
  0.0 116.2 jit_solution(16472858053118718194)
XLA Ops:
  0.6 0.0 copy-start.1
  0.6 2.3 %shard_map.113 = (f32[40,1024]{1,0:T(8,128)}, f32[40,1024]{1,0:T(8,128)}, f32[25,4,1024]{2,1,0:T(4,128)}, f32[25,2,1024]{2,1,0:T(2,128)}, f32[8,128]{1,0:T(8,128)}) custom-call(f32[25,2,4,1024]{3,2,1,0:T(4,128)} %refs_1_.5, f32[25,2,4,1024]{3,2,1,0:T(4,128)} %refs_1_.4, f32[25,2,1024]{2,1,0:T(2,128)} %refs_2_.6, f32[25,2,1024]{2,1,0:T(2,128)} %refs_3_.2), custom_call_target="tpu_custom_call" | custom-call | bytes 2990080 | tf_op jit(solution)/shard_map/pallas_call | solution.py:42
  2.9 1.8 %collective-permute-start.2 = (f32[25,2,1024]{2,1,0:T(2,128)}, f32[25,2,1024]{2,1,0:T(2,128)S(1)}, u32[]{:S(2)}, u32[]{:S(2)}) collective-permute-start(f32[25,2,1024]{2,1,0:T(2,128)} %get-tuple-element.41), channel_id=1, source_target_pairs={{0,32},{32,64},{64,96},{96,128},{128,160},{160,192},{192,224},{1,3... | collective-permute-start | bytes 614408 | tf_op jit(solution)/shard_map/ppermute | solution.py:538
  4.7 3.5 %collective-permute-start = (f32[40,1024]{1,0:T(8,128)}, f32[40,1024]{1,0:T(8,128)S(1)}, u32[]{:S(2)}, u32[]{:S(2)}) collective-permute-start(f32[40,1024]{1,0:T(8,128)} %get-tuple-element.39), channel_id=1, source_target_pairs={{0,1},{1,2},{2,3},{3,4},{4,5},{5,6},{6,7},{7,8},{8,9},{9,10},{10,1... | collective-permute-start | bytes 491528 | tf_op jit(solution)/shard_map/ppermute | solution.py:536
  8.2 2.4 %collective-permute-start.1 = (f32[40,1024]{1,0:T(8,128)}, f32[40,1024]{1,0:T(8,128)S(1)}, u32[]{:S(2)}, u32[]{:S(2)}) collective-permute-start(f32[40,1024]{1,0:T(8,128)} %get-tuple-element.40), channel_id=1, source_target_pairs={{1,0},{2,1},{3,2},{4,3},{5,4},{6,5},{7,6},{8,7},{9,8},{10,9},{11,1... | collective-permute-start | bytes 491528 | tf_op jit(solution)/shard_map/ppermute | solution.py:537
  10.6 0.0 copy-start
  10.6 1.1 copy-done
  11.7 1.1 copy-done.7
  12.8 1.1 copy-done.8
  14.0 0.2 shard_map.112
  14.2 0.0 copy-start.13
  14.2 0.0 collective-permute-done.refs_0_.refs_1_.refs_3_
  14.2 1.4 %collective-permute-done.1.refs_1_.refs_2_.refs_4_ = f32[40,1024]{1,0:T(8,128)S(1)} collective-permute-done((f32[40,1024]{1,0:T(8,128)}, f32[40,1024]{1,0:T(8,128)S(1)}, u32[]{:S(2)}, u32[]{:S(2)}) %collective-permute-start.1) | collective-permute-done | bytes 163872 | tf_op jit(solution)/shard_map/ppermute | solution.py:537
  15.6 4.2 %collective-permute-start.3 = (f32[8,1024]{1,0:T(8,128)S(1)}, f32[8,1024]{1,0:T(8,128)S(1)}, u32[]{:S(2)}, u32[]{:S(2)}) collective-permute-start(f32[8,1024]{1,0:T(8,128)S(1)} %get-tuple-element.43), channel_id=1, source_target_pairs={{0,32},{32,64},{64,96},{96,128},{128,160},{160,192},{192,224},{1,3... | collective-permute-start | bytes 98312 | tf_op jit(solution)/shard_map/ppermute | solution.py:548
  19.8 0.0 copy-done.1
  19.8 0.0 copy-done.2
  19.8 2.2 %shard_map.115 = (f32[25,2,4,1024]{3,2,1,0:T(4,128)S(1)}, f32[25,4,1024]{2,1,0:T(4,128)S(1)}, f32[8,128]{1,0:T(8,128)S(1)}) custom-call(f32[25,2,4,1024]{3,2,1,0:T(4,128)S(1)} %copy-done.1, f32[40,1024]{1,0:T(8,128)S(1)} %collective-permute-done.refs_0_.refs_1_.refs_3_, f32[40,1024]{1,0:T(8,128)S(1)} %collective-permute-done.1.refs_1_.refs_2_.refs_4_, ...), custom_call_target="tpu_custom_call" | custom-call | flops 8192000 | bytes 2785280 | tf_op jit(solution)/shard_map/pallas_call | solution.py:42
  22.1 0.0 collective-permute-done.3.refs_6_
  22.1 0.0 collective-permute-done.2.refs_5_
  22.1 3.2 %shard_map.116 = (f32[25,2,4,1024]{3,2,1,0:T(4,128)S(1)}, f32[25,2,4,1024]{3,2,1,0:T(4,128)S(1)}, f32[25,4,1024]{2,1,0:T(4,128)S(1)}, f32[25,4,1024]{2,1,0:T(4,128)S(1)}, f32[8,128]{1,0:T(8,128)}) custom-call(f32[25,8,1024]{2,1,0:T(8,128)S(1)} %get-tuple-element.36.refs_0_, f32[25,2,4,1024]{3,2,1,0:T(4,128)S(1)} %get-tuple-element.37.refs_1_, ...), custom_call_target="tpu_custom_call" | custom-call | flops 12288000 | bytes 5070848 | tf_op jit(solution)/shard_map/pallas_call | solution.py:42
  25.3 1.4 %collective-permute-start.4 = (f32[25,4,1024]{2,1,0:T(4,128)S(1)}, f32[25,4,1024]{2,1,0:T(4,128)S(1)}, u32[]{:S(2)}, u32[]{:S(2)}) collective-permute-start(f32[25,4,1024]{2,1,0:T(4,128)S(1)} %get-tuple-element.48), channel_id=1, source_target_pairs={{0,32},{32,0},{64,96},{96,64},{128,160},{160,128},{192,224},{224,1... | collective-permute-start | bytes 1228808 | tf_op jit(solution)/shard_map/ppermute | solution.py:565
  26.7 1.4 %collective-permute-done.4.refs_1_.refs_4_ = f32[25,4,1024]{2,1,0:T(4,128)S(1)} collective-permute-done((f32[25,4,1024]{2,1,0:T(4,128)S(1)}, f32[25,4,1024]{2,1,0:T(4,128)S(1)}, u32[]{:S(2)}, u32[]{:S(2)}) %collective-permute-start.4) | collective-permute-done | bytes 409632 | tf_op jit(solution)/shard_map/ppermute | solution.py:565
  28.1 0.1 shard_map.117
  28.2 1.3 %collective-permute-start.5 = (f32[25,4,1024]{2,1,0:T(4,128)S(1)}, f32[25,4,1024]{2,1,0:T(4,128)S(1)}, u32[]{:S(2)}, u32[]{:S(2)}) collective-permute-start(f32[25,4,1024]{2,1,0:T(4,128)S(1)} %get-tuple-element.49), channel_id=1, source_target_pairs={{64,0},{128,64},{192,128},{32,96},{96,160},{160,224},{65,1},{129,6... | collective-permute-start | bytes 1228808 | tf_op jit(solution)/shard_map/ppermute | solution.py:567
  29.5 1.3 %collective-permute-start.6 = (f32[25,4,1024]{2,1,0:T(4,128)S(1)}, f32[25,4,1024]{2,1,0:T(4,128)S(1)}, u32[]{:S(2)}, u32[]{:S(2)}) collective-permute-start(f32[25,4,1024]{2,1,0:T(4,128)S(1)} %get-tuple-element.49), channel_id=1, source_target_pairs={{192,0},{32,224},{193,1},{33,225},{194,2},{34,226},{195,3},{35,227... | collective-permute-start | bytes 1228808 | tf_op jit(solution)/shard_map/ppermute | solution.py:568
  30.8 0.0 copy-done.13
  30.8 2.8 %shard_map.118 = (bf16[400,800]{1,0:T(8,128)(2,1)S(1)}, bf16[400,800]{1,0:T(8,128)(2,1)S(1)}, f32[8,128]{1,0:T(8,128)S(1)}) custom-call(f32[800,800]{1,0:T(8,128)S(1)} %copy-done.13, f32[8,128]{1,0:T(8,128)S(1)} %get-tuple-element.50.refs_1_), custom_call_target="tpu_custom_call" | custom-call | flops 1536000000 | bytes 5120000 | tf_op jit(solution)/shard_map/pallas_call | solution.py:42
  33.5 0.0 copy-start.10
  33.5 0.8 copy-done.10
  34.4 11.9 %collective-permute-done.5.refs_0_ = f32[25,4,1024]{2,1,0:T(4,128)S(1)} collective-permute-done((f32[25,4,1024]{2,1,0:T(4,128)S(1)}, f32[25,4,1024]{2,1,0:T(4,128)S(1)}, u32[]{:S(2)}, u32[]{:S(2)}) %collective-permute-start.5) | collective-permute-done | bytes 409632 | tf_op jit(solution)/shard_map/ppermute | solution.py:567
  46.3 1.3 %collective-permute-start.7 = (f32[25,4,1024]{2,1,0:T(4,128)S(1)}, f32[25,4,1024]{2,1,0:T(4,128)S(1)}, u32[]{:S(2)}, u32[]{:S(2)}) collective-permute-start(f32[25,4,1024]{2,1,0:T(4,128)S(1)} %shard_map.119.refs_1_.refs_0_), channel_id=1, source_target_pairs={{64,0},{128,64},{96,160},{160,224},{65,1},{129,65},{97,161},{161,2... | collective-permute-start | bytes 1228808 | tf_op jit(solution)/shard_map/ppermute | solution.py:584
  47.6 0.0 copy-done.9
  47.6 0.0 copy-start.3
  47.6 0.1 collective-permute-start.9
  47.7 2.8 %shard_map.120 = (bf16[400,800]{1,0:T(8,128)(2,1)S(1)}, bf16[400,800]{1,0:T(8,128)(2,1)S(1)}, f32[8,128]{1,0:T(8,128)S(1)}) custom-call(f32[800,800]{1,0:T(8,128)S(1)} %copy-done.13, f32[25,4,1024]{2,1,0:T(4,128)S(1)} %shard_map.119.refs_1_.refs_0_), custom_call_target="tpu_custom_call" | custom-call | flops 1536000000 | bytes 5120000 | tf_op jit(solution)/shard_map/pallas_call | solution.py:42
  50.5 0.0 copy-start.12
  50.5 0.9 copy-done.12
  51.4 0.0 collective-permute-done.6.refs_1_
  51.4 9.0 %collective-permute-done.7.refs_2_ = f32[25,4,1024]{2,1,0:T(4,128)S(1)} collective-permute-done((f32[25,4,1024]{2,1,0:T(4,128)S(1)}, f32[25,4,1024]{2,1,0:T(4,128)S(1)}, u32[]{:S(2)}, u32[]{:S(2)}) %collective-permute-start.7) | collective-permute-done | bytes 409632 | tf_op jit(solution)/shard_map/ppermute | solution.py:584
  60.4 0.1 shard_map.121
  60.5 0.1 collective-permute-start.8
  60.6 0.0 collective-permute-done.9.refs_7_.refs_5_
  60.6 0.0 copy-done.11
  60.6 0.0 copy-start.5
  60.6 1.7 %collective-permute-done.8.refs_5_ = f32[25,4,1024]{2,1,0:T(4,128)S(1)} collective-permute-done((f32[25,4,1024]{2,1,0:T(4,128)S(1)}, f32[25,4,1024]{2,1,0:T(4,128)S(1)}, u32[]{:S(2)}, u32[]{:S(2)}) %collective-permute-start.8) | collective-permute-done | bytes 409632 | tf_op jit(solution)/shard_map/ppermute | solution.py:591
  62.3 0.0 copy-done.3
  62.3 1.5 %shard_map.122 = (f32[25,2,4,1024]{3,2,1,0:T(4,128)}, f32[32,25,2,128]{3,2,1,0:T(2,128)}, f32[25,4,1024]{2,1,0:T(4,128)S(1)}, f32[8,128]{1,0:T(8,128)}) custom-call(f32[25,2,4,1024]{3,2,1,0:T(4,128)S(1)} %get-tuple-element.45.refs_0_, f32[25,2,4,1024]{3,2,1,0:T(4,128)S(1)} %get-tuple-element.46.refs_1_, f32[25,4,1024]{2,1,0:T(4,128)S(1)} %copy-done.3, ...), custom_call_target="tpu_custom_call" | custom-call | flops 2048000 | bytes 6144000 | tf_op jit(solution)/shard_map/pallas_call | solution.py:42
  63.8 0.0 copy-done.5
  63.8 2.1 %collective-permute-start.10 = (f32[25,4,1024]{2,1,0:T(4,128)S(1)}, f32[25,4,1024]{2,1,0:T(4,128)}, u32[]{:S(2)}, u32[]{:S(2)}) collective-permute-start(f32[25,4,1024]{2,1,0:T(4,128)S(1)} %get-tuple-element.63), channel_id=1, source_target_pairs={{0,192},{32,96},{96,160},{160,224},{1,193},{33,97},{97,161},{161,2... | collective-permute-start | bytes 1228808 | tf_op jit(solution)/shard_map/ppermute | solution.py:610
  65.9 12.8 %all-to-all-start = ((f32[32,25,2,128]{3,2,1,0:T(2,128)}), f32[32,25,2,128]{3,2,1,0:T(2,128)}, u32[]{:S(2)}, u32[]{:S(2)}) async-start(f32[32,25,2,128]{3,2,1,0:T(2,128)} %get-tuple-element.61), calls=%async_computation | async-start | bytes 1638400 | tf_op jit(solution)/shard_map/all_to_all | solution.py:609
  78.7 0.0 collective-permute-done.10.refs_6_.refs_0_
  78.7 1.4 %collective-permute-start.11 = (f32[25,4,1024]{2,1,0:T(4,128)}, f32[25,4,1024]{2,1,0:T(4,128)}, u32[]{:S(2)}, u32[]{:S(2)}) collective-permute-start(f32[25,4,1024]{2,1,0:T(4,128)} %collective-permute-done.10.refs_6_.refs_0_), channel_id=1, source_target_pairs={{96,160},{160,224},{97,161},{161,225},{98,162},{162,226},{99,163},... | collective-permute-start | bytes 1228808 | tf_op jit(solution)/shard_map/ppermute | solution.py:643
  80.2 2.9 %shard_map.123 = (f32[25,2,4,1024]{3,2,1,0:T(4,128)}, f32[8,128]{1,0:T(8,128)}) custom-call(f32[25,2,4,1024]{3,2,1,0:T(4,128)} %refs_0_.11, f32[25,2,4,1024]{3,2,1,0:T(4,128)} %refs_1_.5, f32[25,2,4,1024]{3,2,1,0:T(4,128)} %refs_2_.8, f32[25,2,4,1024]{3,2,1,0:T(4,128)} %refs_3_.3, f32[25,2,4,1024]{3,2,1,0:T(4,128)} %get-tuple-element.33.refs_4_), custom_call_target="tpu_custom_call" | custom-call | flops 99999997952 | bytes 4096000 | tf_op jit(solution)/shard_map/pallas_call | solution.py:42
  83.1 9.5 %all-to-all-done = f32[32,25,2,128]{3,2,1,0:T(2,128)} async-done(((f32[32,25,2,128]{3,2,1,0:T(2,128)}), f32[32,25,2,128]{3,2,1,0:T(2,128)}, u32[]{:S(2)}, u32[]{:S(2)}) %all-to-all-start) | async-done | bytes 819232 | tf_op jit(solution)/shard_map/all_to_all | solution.py:609
  92.6 5.3 %shard_map.124 = (f32[1600,128]{1,0:T(8,128)}, f32[8,128]{1,0:T(8,128)}) custom-call(bf16[400,800]{1,0:T(8,128)(2,1)} %copy-done.9, bf16[400,800]{1,0:T(8,128)(2,1)} %copy-done.10, bf16[400,800]{1,0:T(8,128)(2,1)} %copy-done.11, bf16[400,800]{1,0:T(8,128)(2,1)} %copy-done.12, f32[1600,128]{1,0:T(8,128)} %bitcast.refs_4_, ...), custom_call_target="tpu_custom_call" | custom-call | flops 983040000 | bytes 6758400 | tf_op jit(solution)/shard_map/pallas_call | solution.py:42
  97.9 4.9 %all-to-all-start.1 = ((f32[32,25,2,128]{3,2,1,0:T(2,128)}), f32[32,25,2,128]{3,2,1,0:T(2,128)S(1)}, u32[]{:S(2)}, u32[]{:S(2)}) async-start(f32[32,25,2,128]{3,2,1,0:T(2,128)} %bitcast.2), calls=%async_computation.1 | async-start | bytes 1638400 | tf_op jit(solution)/shard_map/all_to_all | solution.py:639
  102.8 0.0 collective-permute-done.11.refs_1_
  102.8 0.0 copy-start.14
  102.8 0.7 copy-done.14
  103.5 1.3 %shard_map.125 = (f32[25,4,1024]{2,1,0:T(4,128)S(1)}, f32[8,128]{1,0:T(8,128)}) custom-call(f32[25,4,1024]{2,1,0:T(4,128)} %collective-permute-done.10.refs_6_.refs_0_, f32[25,4,1024]{2,1,0:T(4,128)} %collective-permute-done.11.refs_1_, f32[8,128]{1,0:T(8,128)S(1)} %copy-done.14), custom_call_target="tpu_custom_call" | custom-call | flops 99999997952 | bytes 1228800 | tf_op jit(solution)/shard_map/pallas_call | solution.py:42
  104.7 0.1 collective-permute-start.12
  104.8 1.7 %collective-permute-done.12.refs_4_ = f32[25,4,1024]{2,1,0:T(4,128)S(1)} collective-permute-done((f32[25,4,1024]{2,1,0:T(4,128)S(1)}, f32[25,4,1024]{2,1,0:T(4,128)S(1)}, u32[]{:S(2)}, u32[]{:S(2)}) %collective-permute-start.12) | collective-permute-done | bytes 409632 | tf_op jit(solution)/shard_map/ppermute | solution.py:647
  106.6 8.6 %all-to-all-done.1.refs_0_ = f32[32,25,2,128]{3,2,1,0:T(2,128)S(1)} async-done(((f32[32,25,2,128]{3,2,1,0:T(2,128)}), f32[32,25,2,128]{3,2,1,0:T(2,128)S(1)}, u32[]{:S(2)}, u32[]{:S(2)}) %all-to-all-start.1) | async-done | bytes 819232 | tf_op jit(solution)/shard_map/all_to_all | solution.py:639
  115.1 1.1 shard_map.126
  (11 shorter events, 0.0 us)
Async XLA Ops:
  0.6 19.2 %copy-start.1 = (f32[25,2,4,1024]{3,2,1,0:T(4,128)S(1)}, f32[25,2,4,1024]{3,2,1,0:T(4,128)}, u32[]{:S(2)}) copy-start(f32[25,2,4,1024]{3,2,1,0:T(4,128)} %refs_1_.5) | copy-start | bytes 2457604
  2.9 19.1 %collective-permute-start.2 = (f32[25,2,1024]{2,1,0:T(2,128)}, f32[25,2,1024]{2,1,0:T(2,128)S(1)}, u32[]{:S(2)}, u32[]{:S(2)}) collective-permute-start(f32[25,2,1024]{2,1,0:T(2,128)} %get-tuple-element.41), channel_id=1, source_target_pairs={{0,32},{32,64},{64,96},{96,128},{128,160},{160,192},{192,224},{1,3... | collective-permute-start | bytes 614408 | tf_op jit(solution)/shard_map/ppermute | solution.py:538
  4.7 9.5 %collective-permute-start = (f32[40,1024]{1,0:T(8,128)}, f32[40,1024]{1,0:T(8,128)S(1)}, u32[]{:S(2)}, u32[]{:S(2)}) collective-permute-start(f32[40,1024]{1,0:T(8,128)} %get-tuple-element.39), channel_id=1, source_target_pairs={{0,1},{1,2},{2,3},{3,4},{4,5},{5,6},{6,7},{7,8},{8,9},{9,10},{10,1... | collective-permute-start | bytes 491528 | tf_op jit(solution)/shard_map/ppermute | solution.py:536
  8.2 7.4 %collective-permute-start.1 = (f32[40,1024]{1,0:T(8,128)}, f32[40,1024]{1,0:T(8,128)S(1)}, u32[]{:S(2)}, u32[]{:S(2)}) collective-permute-start(f32[40,1024]{1,0:T(8,128)} %get-tuple-element.40), channel_id=1, source_target_pairs={{1,0},{2,1},{3,2},{4,3},{5,4},{6,5},{7,6},{8,7},{9,8},{10,9},{11,1... | collective-permute-start | bytes 491528 | tf_op jit(solution)/shard_map/ppermute | solution.py:537
  10.6 1.1 copy-start
  11.7 1.1 copy-start.7
  12.8 1.1 copy-start.8
  14.0 5.8 %copy-start.2 = (f32[25,4,1024]{2,1,0:T(4,128)S(1)}, f32[25,4,1024]{2,1,0:T(4,128)}, u32[]{:S(2)}) copy-start(f32[25,4,1024]{2,1,0:T(4,128)} %get-tuple-element.38.refs_3_.refs_2_) | copy-start | bytes 1228804
  14.2 16.6 %copy-start.13 = (f32[800,800]{1,0:T(8,128)S(1)}, f32[800,800]{1,0:T(8,128)}, u32[]{:S(2)}) copy-start(f32[800,800]{1,0:T(8,128)} %refs_0_.10) | copy-start | bytes 7680004
  15.6 6.4 %collective-permute-start.3 = (f32[8,1024]{1,0:T(8,128)S(1)}, f32[8,1024]{1,0:T(8,128)S(1)}, u32[]{:S(2)}, u32[]{:S(2)}) collective-permute-start(f32[8,1024]{1,0:T(8,128)S(1)} %get-tuple-element.43), channel_id=1, source_target_pairs={{0,32},{32,64},{64,96},{96,128},{128,160},{160,192},{192,224},{1,3... | collective-permute-start | bytes 98312 | tf_op jit(solution)/shard_map/ppermute | solution.py:548
  25.3 2.8 %collective-permute-start.4 = (f32[25,4,1024]{2,1,0:T(4,128)S(1)}, f32[25,4,1024]{2,1,0:T(4,128)S(1)}, u32[]{:S(2)}, u32[]{:S(2)}) collective-permute-start(f32[25,4,1024]{2,1,0:T(4,128)S(1)} %get-tuple-element.48), channel_id=1, source_target_pairs={{0,32},{32,0},{64,96},{96,64},{128,160},{160,128},{192,224},{224,1... | collective-permute-start | bytes 1228808 | tf_op jit(solution)/shard_map/ppermute | solution.py:565
  28.2 18.2 %collective-permute-start.5 = (f32[25,4,1024]{2,1,0:T(4,128)S(1)}, f32[25,4,1024]{2,1,0:T(4,128)S(1)}, u32[]{:S(2)}, u32[]{:S(2)}) collective-permute-start(f32[25,4,1024]{2,1,0:T(4,128)S(1)} %get-tuple-element.49), channel_id=1, source_target_pairs={{64,0},{128,64},{192,128},{32,96},{96,160},{160,224},{65,1},{129,6... | collective-permute-start | bytes 1228808 | tf_op jit(solution)/shard_map/ppermute | solution.py:567
  29.5 21.9 %collective-permute-start.6 = (f32[25,4,1024]{2,1,0:T(4,128)S(1)}, f32[25,4,1024]{2,1,0:T(4,128)S(1)}, u32[]{:S(2)}, u32[]{:S(2)}) collective-permute-start(f32[25,4,1024]{2,1,0:T(4,128)S(1)} %get-tuple-element.49), channel_id=1, source_target_pairs={{192,0},{32,224},{193,1},{33,225},{194,2},{34,226},{195,3},{35,227... | collective-permute-start | bytes 1228808 | tf_op jit(solution)/shard_map/ppermute | solution.py:568
  33.5 0.8 copy-start.10
  34.4 13.2 %copy-start.9 = (bf16[400,800]{1,0:T(8,128)(2,1)}, bf16[400,800]{1,0:T(8,128)(2,1)S(1)}, u32[]{:S(2)}) copy-start(bf16[400,800]{1,0:T(8,128)(2,1)S(1)} %get-tuple-element.57.refs_0_) | copy-start | bytes 1920004
  46.3 14.1 %collective-permute-start.7 = (f32[25,4,1024]{2,1,0:T(4,128)S(1)}, f32[25,4,1024]{2,1,0:T(4,128)S(1)}, u32[]{:S(2)}, u32[]{:S(2)}) collective-permute-start(f32[25,4,1024]{2,1,0:T(4,128)S(1)} %shard_map.119.refs_1_.refs_0_), channel_id=1, source_target_pairs={{64,0},{128,64},{96,160},{160,224},{65,1},{129,65},{97,161},{161,2... | collective-permute-start | bytes 1228808 | tf_op jit(solution)/shard_map/ppermute | solution.py:584
  47.6 14.7 %copy-start.3 = (f32[25,4,1024]{2,1,0:T(4,128)S(1)}, f32[25,4,1024]{2,1,0:T(4,128)}, u32[]{:S(2)}) copy-start(f32[25,4,1024]{2,1,0:T(4,128)} %refs_2_.9) | copy-start | bytes 1228804
  47.6 13.0 %collective-permute-start.9 = (f32[25,4,1024]{2,1,0:T(4,128)S(1)}, f32[25,4,1024]{2,1,0:T(4,128)S(1)}, u32[]{:S(2)}, u32[]{:S(2)}) collective-permute-start(f32[25,4,1024]{2,1,0:T(4,128)S(1)} %get-tuple-element.54.refs_6_), channel_id=1, source_target_pairs={{0,32},{32,0},{64,96},{96,64},{128,160},{160,128},{192,224},{224,1... | collective-permute-start | bytes 1228808 | tf_op jit(solution)/shard_map/ppermute | solution.py:586
  50.5 0.9 copy-start.12
  51.4 9.2 %copy-start.11 = (bf16[400,800]{1,0:T(8,128)(2,1)}, bf16[400,800]{1,0:T(8,128)(2,1)S(1)}, u32[]{:S(2)}) copy-start(bf16[400,800]{1,0:T(8,128)(2,1)S(1)} %get-tuple-element.59.refs_2_) | copy-start | bytes 1920004
  60.5 1.8 %collective-permute-start.8 = (f32[25,4,1024]{2,1,0:T(4,128)S(1)}, f32[25,4,1024]{2,1,0:T(4,128)S(1)}, u32[]{:S(2)}, u32[]{:S(2)}) collective-permute-start(f32[25,4,1024]{2,1,0:T(4,128)S(1)} %get-tuple-element.53.refs_3_), channel_id=1, source_target_pairs={{0,32},{32,0},{64,96},{96,64},{128,160},{160,128},{192,224},{224,1... | collective-permute-start | bytes 1228808 | tf_op jit(solution)/shard_map/ppermute | solution.py:591
  60.6 3.2 %copy-start.5 = (f32[25,4,1024]{2,1,0:T(4,128)}, f32[25,4,1024]{2,1,0:T(4,128)S(1)}, u32[]{:S(2)}) copy-start(f32[25,4,1024]{2,1,0:T(4,128)S(1)} %collective-permute-done.9.refs_7_.refs_5_) | copy-start | bytes 1228804
  63.8 14.9 %collective-permute-start.10 = (f32[25,4,1024]{2,1,0:T(4,128)S(1)}, f32[25,4,1024]{2,1,0:T(4,128)}, u32[]{:S(2)}, u32[]{:S(2)}) collective-permute-start(f32[25,4,1024]{2,1,0:T(4,128)S(1)} %get-tuple-element.63), channel_id=1, source_target_pairs={{0,192},{32,96},{96,160},{160,224},{1,193},{33,97},{97,161},{161,2... | collective-permute-start | bytes 1228808 | tf_op jit(solution)/shard_map/ppermute | solution.py:610
  65.9 26.7 %all-to-all-start = ((f32[32,25,2,128]{3,2,1,0:T(2,128)}), f32[32,25,2,128]{3,2,1,0:T(2,128)}, u32[]{:S(2)}, u32[]{:S(2)}) async-start(f32[32,25,2,128]{3,2,1,0:T(2,128)} %get-tuple-element.61), calls=%async_computation | async-start | bytes 1638400 | tf_op jit(solution)/shard_map/all_to_all | solution.py:609
  78.7 24.0 %collective-permute-start.11 = (f32[25,4,1024]{2,1,0:T(4,128)}, f32[25,4,1024]{2,1,0:T(4,128)}, u32[]{:S(2)}, u32[]{:S(2)}) collective-permute-start(f32[25,4,1024]{2,1,0:T(4,128)} %collective-permute-done.10.refs_6_.refs_0_), channel_id=1, source_target_pairs={{96,160},{160,224},{97,161},{161,225},{98,162},{162,226},{99,163},... | collective-permute-start | bytes 1228808 | tf_op jit(solution)/shard_map/ppermute | solution.py:643
  97.9 17.3 %all-to-all-start.1 = ((f32[32,25,2,128]{3,2,1,0:T(2,128)}), f32[32,25,2,128]{3,2,1,0:T(2,128)S(1)}, u32[]{:S(2)}, u32[]{:S(2)}) async-start(f32[32,25,2,128]{3,2,1,0:T(2,128)} %bitcast.2), calls=%async_computation.1 | async-start | bytes 1638400 | tf_op jit(solution)/shard_map/all_to_all | solution.py:639
  102.8 0.7 copy-start.14
  103.5 11.7 %copy-start.4 = (f32[25,4,1024]{2,1,0:T(4,128)S(1)}, f32[25,4,1024]{2,1,0:T(4,128)}, u32[]{:S(2)}) copy-start(f32[25,4,1024]{2,1,0:T(4,128)} %refs_2_.9) | copy-start | bytes 1228804
  103.5 11.7 %copy-start.6 = (f32[25,4,1024]{2,1,0:T(4,128)S(1)}, f32[25,4,1024]{2,1,0:T(4,128)}, u32[]{:S(2)}) copy-start(f32[25,4,1024]{2,1,0:T(4,128)} %copy-done.5) | copy-start | bytes 1228804
  104.7 1.8 %collective-permute-start.12 = (f32[25,4,1024]{2,1,0:T(4,128)S(1)}, f32[25,4,1024]{2,1,0:T(4,128)S(1)}, u32[]{:S(2)}, u32[]{:S(2)}) collective-permute-start(f32[25,4,1024]{2,1,0:T(4,128)S(1)} %get-tuple-element.67.refs_3_), channel_id=1, source_target_pairs={{0,32},{32,0},{64,96},{96,64},{128,160},{160,128},{192,224},{224,1... | collective-permute-start | bytes 1228808 | tf_op jit(solution)/shard_map/ppermute | solution.py:647
where the time goes:
time: 118 us; the launch traced here: 116 us
  waiting for transfers between devices  45.3 us (38%)
  starting transfers between devices  38.5 us (33%)
  Pallas kernels  25.6 us (22%)
  local copies, waits for them, and re-layouts  5.84 us (5%)
    pallas_call x14, Pallas kernels, call(): pl.pallas_call(run, out_shape=(*outs, TOKEN), in_specs=[HBM if k in far_i...  25.6 us
    all_to_all x1, starting transfers between devices, body(): lax.all_to_all(columns, 'space', split_axis=0, concat_axis=0, tiled=True)  12.8 us
    ppermute x1, waiting for transfers between devices, body(): near = lax.ppermute(chip_total, 'tm', by_core(fall, rise))  11.9 us
    all_to_all x1, waiting for transfers between devices, body(): lax.all_to_all(columns, 'space', split_axis=0, concat_axis=0, tiled=True)  9.51 us
    ppermute x1, waiting for transfers between devices, body(): on = lax.ppermute(near, 'tm', by_core(fall[:2], rise[1:]))  9.05 us
    all_to_all x1, waiting for transfers between devices, body(): lax.all_to_all(columns.reshape(SPACE, ROWS, 2, LANES), 'space', split_axi...  8.56 us
    unnamed x30, local copies, waits for them, and re-layouts  5.84 us
    all_to_all x1, starting transfers between devices, body(): lax.all_to_all(columns.reshape(SPACE, ROWS, 2, LANES), 'space', split_axi...  4.89 us
  transfers between devices with their start and end apart: 15, of which 8 were waited for; matrix products, arithmetic and copies ran while one was open for 0% of the time, Pallas kernels for 15%

commit v1 on v0

--- a/solution.py
+++ b/solution.py
@@ -187,18 +187,21 @@
 
 
 def filter_kernel(
-    first_high, first_low, second_high, second_low, x_ref, y_ref, high, low, x_high, x_low, y_rows,
-    done, sent,
+    first_high, first_low, second_high, second_low, x_ref, y_ref, high, low, x_rows, x_high,
+    x_low, y_rows, done, sent,
 ):
     copies = [
         pltpu.make_async_copy(source, target.at[pl.ds(block * BLOCK, BLOCK)], done.at[k, block])
         for block, pair in enumerate(((first_high, first_low), (second_high, second_low)))
         for k, (source, target) in enumerate(zip(pair, (high, low)))
     ]
+    arrival = pltpu.make_async_copy(x_ref, x_rows, done.at[2, 0])
+    arrival.start()
     for copy in copies:
         copy.start()
+    arrival.wait()
     for part in range(2):
-        part_high, part_low = split(x_ref[pl.ds(part, LAT, stride=2), :])
+        part_high, part_low = split(x_rows[pl.ds(part, LAT, stride=2), :])
         x_high[:, part * LANES : (part + 1) * LANES] = part_high
         x_low[:, part * LANES : (part + 1) * LANES] = part_low
     for copy in copies:
@@ -546,19 +549,11 @@
     )
     rim, _ = call(rim_kernel, [field(8, LON)], [low, high], after=[token])
     rim = lax.ppermute(rim, "tm", following)
-    model_base, model_total, token = call(
-        tangent_kernel,
-        [whole, half],
-        [increment, low, high, winds],
-        [extended] * 4,
-        flops=40 * ROWS * 8 * LON,
-    )
     dual_base, dual_sums, keep, send, _ = call(
         adjoint_kernel,
         [whole, whole, half, half],
         [own_rows, third, winds, low, high, ahead, rim],
         [extended] * 5,
-        after=[token],
         flops=60 * ROWS * 8 * LON,
     )
 
@@ -580,6 +575,14 @@
         )
 
     first_high, first_low, token = square_half(0, [token])
+    model_base, model_total, token = call(
+        tangent_kernel,
+        [whole, half],
+        [increment, low, high, winds],
+        [extended] * 4,
+        after=[token],
+        flops=40 * ROWS * 8 * LON,
+    )
     near = hold(near, [token])
     on = lax.ppermute(near, "tm", by_core(fall[:2], rise[1:]))
     second_high, second_low, token = square_half(BLOCK, [near])
@@ -627,12 +630,13 @@
         [field(2 * LAT, LANES)],
         [first_high, first_low, second_high, second_low, columns.reshape(2 * LAT, LANES)],
         [square] * 2
+        + [pltpu.VMEM((2 * LAT, LANES), F32)]
         + [pltpu.VMEM((LAT, 2 * LANES), BF16)] * 2
-        + [pltpu.VMEM((2 * LAT, LANES), F32), pltpu.SemaphoreType.DMA((2, LAT // BLOCK))]
+        + [pltpu.VMEM((2 * LAT, LANES), F32), pltpu.SemaphoreType.DMA((3, LAT // BLOCK))]
         + [pltpu.SemaphoreType.DMA((LAT // BLOCK,))],
         after=[token, model_near],
         flops=6 * LAT * LAT * 2 * LANES,
-        far_ins=(0, 1, 2, 3),
+        far_ins=(0, 1, 2, 3, 4),
         far_outs=(0,),
         limit=63 * 1024 * 1024,
     )

time: 118 us -> 117 us (level); the launches traced: 116 us -> 117 us
  starting transfers between devices: 38.5 us -> 39.7 us
    ppermute x1, starting transfers between devices: 2.08 us -> 4.57 us  [body(): model_near = lax.ppermute(model_chip, 'tm', by_core([ends], rise))]
    all_to_all x1, starting transfers between devices: 12.8 us -> 11.1 us  [body(): lax.all_to_all(columns, 'space', split_axis=0, concat_axis=0, tiled=True)]
    ppermute x1, waiting for transfers between devices: 11.9 us -> 10.5 us  [body(): near = lax.ppermute(chip_total, 'tm', by_core(fall, rise))]
  transfers between devices with their start and end apart: 15 -> 15, of which waited for: 8 -> 10; matrix products, arithmetic and copies ran while one was open for 0% -> 0% of each run, Pallas kernels for 15% -> 14%
where the time goes in v1:
time: 117 us
  waiting for transfers between devices  46.3 us (40%)
  starting transfers between devices  39.7 us (34%)
  Pallas kernels  24.6 us (21%)
  local copies, waits for them, and re-layouts  5 us (4%)
    pallas_call x14, Pallas kernels, call(): pl.pallas_call(run, out_shape=(*outs, TOKEN), in_specs=[HBM if k in far_i...  24.6 us
    all_to_all x1, starting transfers between devices, body(): lax.all_to_all(columns, 'space', split_axis=0, concat_axis=0, tiled=True)  11.1 us
    ppermute x1, waiting for transfers between devices, body(): near = lax.ppermute(chip_total, 'tm', by_core(fall, rise))  10.5 us
    all_to_all x1, waiting for transfers between devices, body(): lax.all_to_all(columns, 'space', split_axis=0, concat_axis=0, tiled=True)  10.1 us
    all_to_all x1, waiting for transfers between devices, body(): lax.all_to_all(columns.reshape(SPACE, ROWS, 2, LANES), 'space', split_axi...  9.55 us
    ppermute x1, waiting for transfers between devices, body(): on = lax.ppermute(near, 'tm', by_core(fall[:2], rise[1:]))  8.66 us
    all_to_all x1, starting transfers between devices, body(): lax.all_to_all(columns.reshape(SPACE, ROWS, 2, LANES), 'space', split_axi...  5.09 us
    unnamed x30, local copies, waits for them, and re-layouts  5 us
  transfers between devices with their start and end apart: 15, of which 10 were waited for; matrix products, arithmetic and copies ran while one was open for 0% of the time, Pallas kernels for 14%

profile of v1, /device:TPU:8, one launch (start us, length us, event | category | flops | bytes accessed | tf_op | source)
XLA Modules:
  0.0 116.6 jit_solution(2215119011237818681)
XLA Ops:
  0.6 2.2 %shard_map.113 = (f32[40,1024]{1,0:T(8,128)}, f32[40,1024]{1,0:T(8,128)}, f32[25,4,1024]{2,1,0:T(4,128)}, f32[25,2,1024]{2,1,0:T(2,128)}, f32[8,128]{1,0:T(8,128)}) custom-call(f32[25,2,4,1024]{3,2,1,0:T(4,128)} %refs_1_.5, f32[25,2,4,1024]{3,2,1,0:T(4,128)} %refs_1_.4, f32[25,2,1024]{2,1,0:T(2,128)} %refs_2_.6, f32[25,2,1024]{2,1,0:T(2,128)} %refs_3_.2), custom_call_target="tpu_custom_call" | custom-call | bytes 2990080 | tf_op jit(solution)/shard_map/pallas_call | solution.py:42
  2.8 1.8 %collective-permute-start.2 = (f32[25,2,1024]{2,1,0:T(2,128)}, f32[25,2,1024]{2,1,0:T(2,128)S(1)}, u32[]{:S(2)}, u32[]{:S(2)}) collective-permute-start(f32[25,2,1024]{2,1,0:T(2,128)} %get-tuple-element.41), channel_id=1, source_target_pairs={{0,32},{32,64},{64,96},{96,128},{128,160},{160,192},{192,224},{1,3... | collective-permute-start | bytes 614408 | tf_op jit(solution)/shard_map/ppermute | solution.py:541
  4.6 3.5 %collective-permute-start = (f32[40,1024]{1,0:T(8,128)}, f32[40,1024]{1,0:T(8,128)S(1)}, u32[]{:S(2)}, u32[]{:S(2)}) collective-permute-start(f32[40,1024]{1,0:T(8,128)} %get-tuple-element.39), channel_id=1, source_target_pairs={{0,1},{1,2},{2,3},{3,4},{4,5},{5,6},{6,7},{7,8},{8,9},{9,10},{10,1... | collective-permute-start | bytes 491528 | tf_op jit(solution)/shard_map/ppermute | solution.py:539
  8.1 2.4 %collective-permute-start.1 = (f32[40,1024]{1,0:T(8,128)}, f32[40,1024]{1,0:T(8,128)S(1)}, u32[]{:S(2)}, u32[]{:S(2)}) collective-permute-start(f32[40,1024]{1,0:T(8,128)} %get-tuple-element.40), channel_id=1, source_target_pairs={{1,0},{2,1},{3,2},{4,3},{5,4},{6,5},{7,6},{8,7},{9,8},{10,9},{11,1... | collective-permute-start | bytes 491528 | tf_op jit(solution)/shard_map/ppermute | solution.py:540
  10.5 0.0 copy-start
  10.5 1.1 copy-done
  11.6 1.1 copy-done.7
  12.8 1.1 copy-done.8
  13.9 0.2 shard_map.112
  14.1 0.0 collective-permute-done.refs_0_.refs_3_.refs_1_
  14.1 1.4 %collective-permute-done.1.refs_1_.refs_4_.refs_2_ = f32[40,1024]{1,0:T(8,128)S(1)} collective-permute-done((f32[40,1024]{1,0:T(8,128)}, f32[40,1024]{1,0:T(8,128)S(1)}, u32[]{:S(2)}, u32[]{:S(2)}) %collective-permute-start.1) | collective-permute-done | bytes 163872 | tf_op jit(solution)/shard_map/ppermute | solution.py:540
  15.5 4.2 %collective-permute-start.3 = (f32[8,1024]{1,0:T(8,128)S(1)}, f32[8,1024]{1,0:T(8,128)S(1)}, u32[]{:S(2)}, u32[]{:S(2)}) collective-permute-start(f32[8,1024]{1,0:T(8,128)S(1)} %get-tuple-element.43), channel_id=1, source_target_pairs={{0,32},{32,64},{64,96},{96,128},{128,160},{160,192},{192,224},{1,3... | collective-permute-start | bytes 98312 | tf_op jit(solution)/shard_map/ppermute | solution.py:551
  19.7 0.8 collective-permute-done.3.refs_6_
  20.5 0.0 collective-permute-done.2.refs_5_
  20.5 0.0 copy-done.2
  20.5 3.2 %shard_map.115 = (f32[25,2,4,1024]{3,2,1,0:T(4,128)S(1)}, f32[25,2,4,1024]{3,2,1,0:T(4,128)S(1)}, f32[25,4,1024]{2,1,0:T(4,128)S(1)}, f32[25,4,1024]{2,1,0:T(4,128)S(1)}, f32[8,128]{1,0:T(8,128)}) custom-call(f32[25,8,1024]{2,1,0:T(8,128)S(1)} %get-tuple-element.36.refs_0_, f32[25,2,4,1024]{3,2,1,0:T(4,128)S(1)} %get-tuple-element.37.refs_1_, ...), custom_call_target="tpu_custom_call" | custom-call | flops 12288000 | bytes 5070848 | tf_op jit(solution)/shard_map/pallas_call | solution.py:42
  23.8 1.6 %collective-permute-start.4 = (f32[25,4,1024]{2,1,0:T(4,128)S(1)}, f32[25,4,1024]{2,1,0:T(4,128)S(1)}, u32[]{:S(2)}, u32[]{:S(2)}) collective-permute-start(f32[25,4,1024]{2,1,0:T(4,128)S(1)} %get-tuple-element.47), channel_id=1, source_target_pairs={{0,32},{32,0},{64,96},{96,64},{128,160},{160,128},{192,224},{224,1... | collective-permute-start | bytes 1228808 | tf_op jit(solution)/shard_map/ppermute | solution.py:560
  25.3 1.4 %collective-permute-done.4.refs_1_.refs_4_ = f32[25,4,1024]{2,1,0:T(4,128)S(1)} collective-permute-done((f32[25,4,1024]{2,1,0:T(4,128)S(1)}, f32[25,4,1024]{2,1,0:T(4,128)S(1)}, u32[]{:S(2)}, u32[]{:S(2)}) %collective-permute-start.4) | collective-permute-done | bytes 409632 | tf_op jit(solution)/shard_map/ppermute | solution.py:560
  26.7 0.1 shard_map.116
  26.8 0.0 copy-start.1
  26.8 1.4 %collective-permute-start.5 = (f32[25,4,1024]{2,1,0:T(4,128)S(1)}, f32[25,4,1024]{2,1,0:T(4,128)S(1)}, u32[]{:S(2)}, u32[]{:S(2)}) collective-permute-start(f32[25,4,1024]{2,1,0:T(4,128)S(1)} %get-tuple-element.48), channel_id=1, source_target_pairs={{64,0},{128,64},{192,128},{32,96},{96,160},{160,224},{65,1},{129,6... | collective-permute-start | bytes 1228808 | tf_op jit(solution)/shard_map/ppermute | solution.py:562
  28.2 1.3 %collective-permute-start.6 = (f32[25,4,1024]{2,1,0:T(4,128)S(1)}, f32[25,4,1024]{2,1,0:T(4,128)S(1)}, u32[]{:S(2)}, u32[]{:S(2)}) collective-permute-start(f32[25,4,1024]{2,1,0:T(4,128)S(1)} %get-tuple-element.48), channel_id=1, source_target_pairs={{192,0},{32,224},{193,1},{33,225},{194,2},{34,226},{195,3},{35,227... | collective-permute-start | bytes 1228808 | tf_op jit(solution)/shard_map/ppermute | solution.py:563
  29.5 0.0 copy-done.13
  29.5 2.8 %shard_map.117 = (bf16[400,800]{1,0:T(8,128)(2,1)S(1)}, bf16[400,800]{1,0:T(8,128)(2,1)S(1)}, f32[8,128]{1,0:T(8,128)S(1)}) custom-call(f32[800,800]{1,0:T(8,128)S(1)} %copy-done.13, f32[8,128]{1,0:T(8,128)S(1)} %get-tuple-element.49.refs_1_), custom_call_target="tpu_custom_call" | custom-call | flops 1536000000 | bytes 5120000 | tf_op jit(solution)/shard_map/pallas_call | solution.py:42
  32.3 0.0 copy-start.9
  32.3 0.0 copy-start.10
  32.3 0.0 copy-done.1
  32.3 2.3 %shard_map.118 = (f32[25,2,4,1024]{3,2,1,0:T(4,128)S(1)}, f32[25,4,1024]{2,1,0:T(4,128)S(1)}, f32[8,128]{1,0:T(8,128)S(1)}) custom-call(f32[25,2,4,1024]{3,2,1,0:T(4,128)S(1)} %copy-done.1, f32[40,1024]{1,0:T(8,128)S(1)} %collective-permute-done.refs_0_.refs_3_.refs_1_, f32[40,1024]{1,0:T(8,128)S(1)} %collective-permute-done.1.refs_1_.refs_4_.refs_2_, ...), custom_call_target="tpu_custom_call" | custom-call | flops 8192000 | bytes 2785280 | tf_op jit(solution)/shard_map/pallas_call | solution.py:42
  34.6 10.5 %collective-permute-done.5.refs_0_ = f32[25,4,1024]{2,1,0:T(4,128)S(1)} collective-permute-done((f32[25,4,1024]{2,1,0:T(4,128)S(1)}, f32[25,4,1024]{2,1,0:T(4,128)S(1)}, u32[]{:S(2)}, u32[]{:S(2)}) %collective-permute-start.5) | collective-permute-done | bytes 409632 | tf_op jit(solution)/shard_map/ppermute | solution.py:562
  45.1 1.3 %collective-permute-start.7 = (f32[25,4,1024]{2,1,0:T(4,128)S(1)}, f32[25,4,1024]{2,1,0:T(4,128)S(1)}, u32[]{:S(2)}, u32[]{:S(2)}) collective-permute-start(f32[25,4,1024]{2,1,0:T(4,128)S(1)} %shard_map.119.refs_1_.refs_0_), channel_id=1, source_target_pairs={{64,0},{128,64},{96,160},{160,224},{65,1},{129,65},{97,161},{161,2... | collective-permute-start | bytes 1228808 | tf_op jit(solution)/shard_map/ppermute | solution.py:587
  46.4 0.0 copy-done.9
  46.4 0.0 copy-done.10
  46.4 0.0 copy-start.3
  46.5 0.1 collective-permute-start.9
  46.6 2.8 %shard_map.120 = (bf16[400,800]{1,0:T(8,128)(2,1)S(1)}, bf16[400,800]{1,0:T(8,128)(2,1)S(1)}, f32[8,128]{1,0:T(8,128)S(1)}) custom-call(f32[800,800]{1,0:T(8,128)S(1)} %copy-done.13, f32[25,4,1024]{2,1,0:T(4,128)S(1)} %shard_map.119.refs_1_.refs_0_), custom_call_target="tpu_custom_call" | custom-call | flops 1536000000 | bytes 5120000 | tf_op jit(solution)/shard_map/pallas_call | solution.py:42
  49.3 0.0 copy-start.12
  49.3 0.9 copy-done.12
  50.2 0.4 collective-permute-done.6.refs_1_
  50.6 8.7 %collective-permute-done.7.refs_2_ = f32[25,4,1024]{2,1,0:T(4,128)S(1)} collective-permute-done((f32[25,4,1024]{2,1,0:T(4,128)S(1)}, f32[25,4,1024]{2,1,0:T(4,128)S(1)}, u32[]{:S(2)}, u32[]{:S(2)}) %collective-permute-start.7) | collective-permute-done | bytes 409632 | tf_op jit(solution)/shard_map/ppermute | solution.py:587
  59.2 0.1 shard_map.121
  59.3 0.1 collective-permute-start.8
  59.4 0.0 collective-permute-done.9.refs_7_.refs_5_
  59.4 0.0 copy-done.11
  59.4 0.0 copy-start.5
  59.5 1.7 %collective-permute-done.8.refs_5_ = f32[25,4,1024]{2,1,0:T(4,128)S(1)} collective-permute-done((f32[25,4,1024]{2,1,0:T(4,128)S(1)}, f32[25,4,1024]{2,1,0:T(4,128)S(1)}, u32[]{:S(2)}, u32[]{:S(2)}) %collective-permute-start.8) | collective-permute-done | bytes 409632 | tf_op jit(solution)/shard_map/ppermute | solution.py:594
  61.2 0.0 copy-done.3
  61.2 1.5 %shard_map.122 = (f32[25,2,4,1024]{3,2,1,0:T(4,128)}, f32[32,25,2,128]{3,2,1,0:T(2,128)}, f32[25,4,1024]{2,1,0:T(4,128)S(1)}, f32[8,128]{1,0:T(8,128)}) custom-call(f32[25,2,4,1024]{3,2,1,0:T(4,128)S(1)} %get-tuple-element.44.refs_0_, f32[25,2,4,1024]{3,2,1,0:T(4,128)S(1)} %get-tuple-element.45.refs_1_, f32[25,4,1024]{2,1,0:T(4,128)S(1)} %copy-done.3, ...), custom_call_target="tpu_custom_call" | custom-call | flops 2048000 | bytes 6144000 | tf_op jit(solution)/shard_map/pallas_call | solution.py:42
  62.6 4.6 %collective-permute-start.10 = (f32[25,4,1024]{2,1,0:T(4,128)S(1)}, f32[25,4,1024]{2,1,0:T(4,128)}, u32[]{:S(2)}, u32[]{:S(2)}) collective-permute-start(f32[25,4,1024]{2,1,0:T(4,128)S(1)} %get-tuple-element.63), channel_id=1, source_target_pairs={{0,192},{32,96},{96,160},{160,224},{1,193},{33,97},{97,161},{161,2... | collective-permute-start | bytes 1228808 | tf_op jit(solution)/shard_map/ppermute | solution.py:613
  67.2 11.1 %all-to-all-start = ((f32[32,25,2,128]{3,2,1,0:T(2,128)}), f32[32,25,2,128]{3,2,1,0:T(2,128)}, u32[]{:S(2)}, u32[]{:S(2)}) async-start(f32[32,25,2,128]{3,2,1,0:T(2,128)} %get-tuple-element.61), calls=%async_computation | async-start | bytes 1638400 | tf_op jit(solution)/shard_map/all_to_all | solution.py:612
  78.3 0.0 collective-permute-done.10.refs_6_.refs_0_
  78.3 1.4 %collective-permute-start.11 = (f32[25,4,1024]{2,1,0:T(4,128)}, f32[25,4,1024]{2,1,0:T(4,128)}, u32[]{:S(2)}, u32[]{:S(2)}) collective-permute-start(f32[25,4,1024]{2,1,0:T(4,128)} %collective-permute-done.10.refs_6_.refs_0_), channel_id=1, source_target_pairs={{96,160},{160,224},{97,161},{161,225},{98,162},{162,226},{99,163},... | collective-permute-start | bytes 1228808 | tf_op jit(solution)/shard_map/ppermute | solution.py:647
  79.7 2.9 %shard_map.123 = (f32[25,2,4,1024]{3,2,1,0:T(4,128)}, f32[8,128]{1,0:T(8,128)}) custom-call(f32[25,2,4,1024]{3,2,1,0:T(4,128)} %refs_0_.11, f32[25,2,4,1024]{3,2,1,0:T(4,128)} %refs_1_.5, f32[25,2,4,1024]{3,2,1,0:T(4,128)} %refs_2_.8, f32[25,2,4,1024]{3,2,1,0:T(4,128)} %refs_3_.3, f32[25,2,4,1024]{3,2,1,0:T(4,128)} %get-tuple-element.33.refs_4_), custom_call_target="tpu_custom_call" | custom-call | flops 99999997952 | bytes 4096000 | tf_op jit(solution)/shard_map/pallas_call | solution.py:42
  82.6 10.1 %all-to-all-done = f32[32,25,2,128]{3,2,1,0:T(2,128)} async-done(((f32[32,25,2,128]{3,2,1,0:T(2,128)}), f32[32,25,2,128]{3,2,1,0:T(2,128)}, u32[]{:S(2)}, u32[]{:S(2)}) %all-to-all-start) | async-done | bytes 819232 | tf_op jit(solution)/shard_map/all_to_all | solution.py:612
  92.7 4.4 %shard_map.124 = (f32[1600,128]{1,0:T(8,128)}, f32[8,128]{1,0:T(8,128)}) custom-call(bf16[400,800]{1,0:T(8,128)(2,1)} %copy-done.9, bf16[400,800]{1,0:T(8,128)(2,1)} %copy-done.10, bf16[400,800]{1,0:T(8,128)(2,1)} %copy-done.11, bf16[400,800]{1,0:T(8,128)(2,1)} %copy-done.12, f32[1600,128]{1,0:T(8,128)} %bitcast.refs_4_, ...), custom_call_target="tpu_custom_call" | custom-call | flops 983040000 | bytes 6758400 | tf_op jit(solution)/shard_map/pallas_call | solution.py:42
  97.1 5.1 %all-to-all-start.1 = ((f32[32,25,2,128]{3,2,1,0:T(2,128)}), f32[32,25,2,128]{3,2,1,0:T(2,128)S(1)}, u32[]{:S(2)}, u32[]{:S(2)}) async-start(f32[32,25,2,128]{3,2,1,0:T(2,128)} %bitcast.2), calls=%async_computation.1 | async-start | bytes 1638400 | tf_op jit(solution)/shard_map/all_to_all | solution.py:643
  102.2 0.0 collective-permute-done.11.refs_1_
  102.2 0.0 copy-start.14
  102.3 0.7 copy-done.14
  102.9 1.3 %shard_map.125 = (f32[25,4,1024]{2,1,0:T(4,128)S(1)}, f32[8,128]{1,0:T(8,128)}) custom-call(f32[25,4,1024]{2,1,0:T(4,128)} %collective-permute-done.10.refs_6_.refs_0_, f32[25,4,1024]{2,1,0:T(4,128)} %collective-permute-done.11.refs_1_, f32[8,128]{1,0:T(8,128)S(1)} %copy-done.14), custom_call_target="tpu_custom_call" | custom-call | flops 99999997952 | bytes 1228800 | tf_op jit(solution)/shard_map/pallas_call | solution.py:42
  104.2 0.1 collective-permute-start.12
  104.3 1.7 %collective-permute-done.12.refs_4_ = f32[25,4,1024]{2,1,0:T(4,128)S(1)} collective-permute-done((f32[25,4,1024]{2,1,0:T(4,128)S(1)}, f32[25,4,1024]{2,1,0:T(4,128)S(1)}, u32[]{:S(2)}, u32[]{:S(2)}) %collective-permute-start.12) | collective-permute-done | bytes 409632 | tf_op jit(solution)/shard_map/ppermute | solution.py:651
  106.0 9.6 %all-to-all-done.1.refs_0_ = f32[32,25,2,128]{3,2,1,0:T(2,128)S(1)} async-done(((f32[32,25,2,128]{3,2,1,0:T(2,128)}), f32[32,25,2,128]{3,2,1,0:T(2,128)S(1)}, u32[]{:S(2)}, u32[]{:S(2)}) %all-to-all-start.1) | async-done | bytes 819232 | tf_op jit(solution)/shard_map/all_to_all | solution.py:643
  115.6 0.0 copy-done.6
  115.6 1.1 shard_map.126
  (11 shorter events, 0.0 us)
Async XLA Ops:
  2.8 17.7 %collective-permute-start.2 = (f32[25,2,1024]{2,1,0:T(2,128)}, f32[25,2,1024]{2,1,0:T(2,128)S(1)}, u32[]{:S(2)}, u32[]{:S(2)}) collective-permute-start(f32[25,2,1024]{2,1,0:T(2,128)} %get-tuple-element.41), channel_id=1, source_target_pairs={{0,32},{32,64},{64,96},{96,128},{128,160},{160,192},{192,224},{1,3... | collective-permute-start | bytes 614408 | tf_op jit(solution)/shard_map/ppermute | solution.py:541
  4.6 9.5 %collective-permute-start = (f32[40,1024]{1,0:T(8,128)}, f32[40,1024]{1,0:T(8,128)S(1)}, u32[]{:S(2)}, u32[]{:S(2)}) collective-permute-start(f32[40,1024]{1,0:T(8,128)} %get-tuple-element.39), channel_id=1, source_target_pairs={{0,1},{1,2},{2,3},{3,4},{4,5},{5,6},{6,7},{7,8},{8,9},{9,10},{10,1... | collective-permute-start | bytes 491528 | tf_op jit(solution)/shard_map/ppermute | solution.py:539
  8.1 7.4 %collective-permute-start.1 = (f32[40,1024]{1,0:T(8,128)}, f32[40,1024]{1,0:T(8,128)S(1)}, u32[]{:S(2)}, u32[]{:S(2)}) collective-permute-start(f32[40,1024]{1,0:T(8,128)} %get-tuple-element.40), channel_id=1, source_target_pairs={{1,0},{2,1},{3,2},{4,3},{5,4},{6,5},{7,6},{8,7},{9,8},{10,9},{11,1... | collective-permute-start | bytes 491528 | tf_op jit(solution)/shard_map/ppermute | solution.py:540
  10.5 1.1 copy-start
  11.6 1.1 copy-start.7
  12.8 1.1 copy-start.8
  13.9 6.6 %copy-start.2 = (f32[25,4,1024]{2,1,0:T(4,128)S(1)}, f32[25,4,1024]{2,1,0:T(4,128)}, u32[]{:S(2)}) copy-start(f32[25,4,1024]{2,1,0:T(4,128)} %get-tuple-element.38.refs_2_.refs_3_) | copy-start | bytes 1228804
  13.9 15.6 %copy-start.13 = (f32[800,800]{1,0:T(8,128)S(1)}, f32[800,800]{1,0:T(8,128)}, u32[]{:S(2)}) copy-start(f32[800,800]{1,0:T(8,128)} %refs_0_.10) | copy-start | bytes 7680004
  15.5 5.0 %collective-permute-start.3 = (f32[8,1024]{1,0:T(8,128)S(1)}, f32[8,1024]{1,0:T(8,128)S(1)}, u32[]{:S(2)}, u32[]{:S(2)}) collective-permute-start(f32[8,1024]{1,0:T(8,128)S(1)} %get-tuple-element.43), channel_id=1, source_target_pairs={{0,32},{32,64},{64,96},{96,128},{128,160},{160,192},{192,224},{1,3... | collective-permute-start | bytes 98312 | tf_op jit(solution)/shard_map/ppermute | solution.py:551
  23.8 2.9 %collective-permute-start.4 = (f32[25,4,1024]{2,1,0:T(4,128)S(1)}, f32[25,4,1024]{2,1,0:T(4,128)S(1)}, u32[]{:S(2)}, u32[]{:S(2)}) collective-permute-start(f32[25,4,1024]{2,1,0:T(4,128)S(1)} %get-tuple-element.47), channel_id=1, source_target_pairs={{0,32},{32,0},{64,96},{96,64},{128,160},{160,128},{192,224},{224,1... | collective-permute-start | bytes 1228808 | tf_op jit(solution)/shard_map/ppermute | solution.py:560
  26.8 5.6 %copy-start.1 = (f32[25,2,4,1024]{3,2,1,0:T(4,128)S(1)}, f32[25,2,4,1024]{3,2,1,0:T(4,128)}, u32[]{:S(2)}) copy-start(f32[25,2,4,1024]{3,2,1,0:T(4,128)} %refs_1_.5) | copy-start | bytes 2457604
  26.8 18.4 %collective-permute-start.5 = (f32[25,4,1024]{2,1,0:T(4,128)S(1)}, f32[25,4,1024]{2,1,0:T(4,128)S(1)}, u32[]{:S(2)}, u32[]{:S(2)}) collective-permute-start(f32[25,4,1024]{2,1,0:T(4,128)S(1)} %get-tuple-element.48), channel_id=1, source_target_pairs={{64,0},{128,64},{192,128},{32,96},{96,160},{160,224},{65,1},{129,6... | collective-permute-start | bytes 1228808 | tf_op jit(solution)/shard_map/ppermute | solution.py:562
  28.2 22.4 %collective-permute-start.6 = (f32[25,4,1024]{2,1,0:T(4,128)S(1)}, f32[25,4,1024]{2,1,0:T(4,128)S(1)}, u32[]{:S(2)}, u32[]{:S(2)}) collective-permute-start(f32[25,4,1024]{2,1,0:T(4,128)S(1)} %get-tuple-element.48), channel_id=1, source_target_pairs={{192,0},{32,224},{193,1},{33,225},{194,2},{34,226},{195,3},{35,227... | collective-permute-start | bytes 1228808 | tf_op jit(solution)/shard_map/ppermute | solution.py:563
  32.3 14.1 %copy-start.9 = (bf16[400,800]{1,0:T(8,128)(2,1)}, bf16[400,800]{1,0:T(8,128)(2,1)S(1)}, u32[]{:S(2)}) copy-start(bf16[400,800]{1,0:T(8,128)(2,1)S(1)} %get-tuple-element.57.refs_0_) | copy-start | bytes 1920004
  32.3 14.1 %copy-start.10 = (bf16[400,800]{1,0:T(8,128)(2,1)}, bf16[400,800]{1,0:T(8,128)(2,1)S(1)}, u32[]{:S(2)}) copy-start(bf16[400,800]{1,0:T(8,128)(2,1)S(1)} %get-tuple-element.58.refs_1_) | copy-start | bytes 1920004
  45.1 14.1 %collective-permute-start.7 = (f32[25,4,1024]{2,1,0:T(4,128)S(1)}, f32[25,4,1024]{2,1,0:T(4,128)S(1)}, u32[]{:S(2)}, u32[]{:S(2)}) collective-permute-start(f32[25,4,1024]{2,1,0:T(4,128)S(1)} %shard_map.119.refs_1_.refs_0_), channel_id=1, source_target_pairs={{64,0},{128,64},{96,160},{160,224},{65,1},{129,65},{97,161},{161,2... | collective-permute-start | bytes 1228808 | tf_op jit(solution)/shard_map/ppermute | solution.py:587
  46.4 14.7 %copy-start.3 = (f32[25,4,1024]{2,1,0:T(4,128)S(1)}, f32[25,4,1024]{2,1,0:T(4,128)}, u32[]{:S(2)}) copy-start(f32[25,4,1024]{2,1,0:T(4,128)} %refs_2_.9) | copy-start | bytes 1228804
  46.5 13.0 %collective-permute-start.9 = (f32[25,4,1024]{2,1,0:T(4,128)S(1)}, f32[25,4,1024]{2,1,0:T(4,128)S(1)}, u32[]{:S(2)}, u32[]{:S(2)}) collective-permute-start(f32[25,4,1024]{2,1,0:T(4,128)S(1)} %get-tuple-element.54.refs_6_), channel_id=1, source_target_pairs={{0,32},{32,0},{64,96},{96,64},{128,160},{160,128},{192,224},{224,1... | collective-permute-start | bytes 1228808 | tf_op jit(solution)/shard_map/ppermute | solution.py:589
  49.3 0.9 copy-start.12
  50.2 9.3 %copy-start.11 = (bf16[400,800]{1,0:T(8,128)(2,1)}, bf16[400,800]{1,0:T(8,128)(2,1)S(1)}, u32[]{:S(2)}) copy-start(bf16[400,800]{1,0:T(8,128)(2,1)S(1)} %get-tuple-element.59.refs_2_) | copy-start | bytes 1920004
  59.3 1.8 %collective-permute-start.8 = (f32[25,4,1024]{2,1,0:T(4,128)S(1)}, f32[25,4,1024]{2,1,0:T(4,128)S(1)}, u32[]{:S(2)}, u32[]{:S(2)}) collective-permute-start(f32[25,4,1024]{2,1,0:T(4,128)S(1)} %get-tuple-element.53.refs_3_), channel_id=1, source_target_pairs={{0,32},{32,0},{64,96},{96,64},{128,160},{160,128},{192,224},{224,1... | collective-permute-start | bytes 1228808 | tf_op jit(solution)/shard_map/ppermute | solution.py:594
  59.4 3.2 %copy-start.5 = (f32[25,4,1024]{2,1,0:T(4,128)}, f32[25,4,1024]{2,1,0:T(4,128)S(1)}, u32[]{:S(2)}) copy-start(f32[25,4,1024]{2,1,0:T(4,128)S(1)} %collective-permute-done.9.refs_7_.refs_5_) | copy-start | bytes 1228804
  62.6 15.6 %collective-permute-start.10 = (f32[25,4,1024]{2,1,0:T(4,128)S(1)}, f32[25,4,1024]{2,1,0:T(4,128)}, u32[]{:S(2)}, u32[]{:S(2)}) collective-permute-start(f32[25,4,1024]{2,1,0:T(4,128)S(1)} %get-tuple-element.63), channel_id=1, source_target_pairs={{0,192},{32,96},{96,160},{160,224},{1,193},{33,97},{97,161},{161,2... | collective-permute-start | bytes 1228808 | tf_op jit(solution)/shard_map/ppermute | solution.py:613
  67.2 25.5 %all-to-all-start = ((f32[32,25,2,128]{3,2,1,0:T(2,128)}), f32[32,25,2,128]{3,2,1,0:T(2,128)}, u32[]{:S(2)}, u32[]{:S(2)}) async-start(f32[32,25,2,128]{3,2,1,0:T(2,128)} %get-tuple-element.61), calls=%async_computation | async-start | bytes 1638400 | tf_op jit(solution)/shard_map/all_to_all | solution.py:612
  78.3 23.9 %collective-permute-start.11 = (f32[25,4,1024]{2,1,0:T(4,128)}, f32[25,4,1024]{2,1,0:T(4,128)}, u32[]{:S(2)}, u32[]{:S(2)}) collective-permute-start(f32[25,4,1024]{2,1,0:T(4,128)} %collective-permute-done.10.refs_6_.refs_0_), channel_id=1, source_target_pairs={{96,160},{160,224},{97,161},{161,225},{98,162},{162,226},{99,163},... | collective-permute-start | bytes 1228808 | tf_op jit(solution)/shard_map/ppermute | solution.py:647
  97.1 18.4 %all-to-all-start.1 = ((f32[32,25,2,128]{3,2,1,0:T(2,128)}), f32[32,25,2,128]{3,2,1,0:T(2,128)S(1)}, u32[]{:S(2)}, u32[]{:S(2)}) async-start(f32[32,25,2,128]{3,2,1,0:T(2,128)} %bitcast.2), calls=%async_computation.1 | async-start | bytes 1638400 | tf_op jit(solution)/shard_map/all_to_all | solution.py:643
  102.2 0.7 copy-start.14
  102.9 12.7 %copy-start.4 = (f32[25,4,1024]{2,1,0:T(4,128)S(1)}, f32[25,4,1024]{2,1,0:T(4,128)}, u32[]{:S(2)}) copy-start(f32[25,4,1024]{2,1,0:T(4,128)} %refs_2_.9) | copy-start | bytes 1228804
  102.9 12.7 %copy-start.6 = (f32[25,4,1024]{2,1,0:T(4,128)S(1)}, f32[25,4,1024]{2,1,0:T(4,128)}, u32[]{:S(2)}) copy-start(f32[25,4,1024]{2,1,0:T(4,128)} %copy-done.5) | copy-start | bytes 1228804
  104.2 1.8 %collective-permute-start.12 = (f32[25,4,1024]{2,1,0:T(4,128)S(1)}, f32[25,4,1024]{2,1,0:T(4,128)S(1)}, u32[]{:S(2)}, u32[]{:S(2)}) collective-permute-start(f32[25,4,1024]{2,1,0:T(4,128)S(1)} %get-tuple-element.67.refs_3_), channel_id=1, source_target_pairs={{0,32},{32,0},{64,96},{96,64},{128,160},{160,128},{192,224},{224,1... | collective-permute-start | bytes 1228808 | tf_op jit(solution)/shard_map/ppermute | solution.py:651
